TPU v7x, 32 devices: a whole 2x2x4 slice. The times are simulated.
32 devices in a mesh: aux: 4 (over z), ao: 8 (over y, x, core).
Axes of the slice: x: 2, y: 2, z: 4, core: 2. Of those that a mesh axis runs over, the one named last changes fastest.
Arguments:
- tensor: bfloat16 [64, 1024, 1024], P('aux', 'ao'), may hold values from -6 to 6
- green: bfloat16 [1024, 1024], P('aux', 'ao'), may hold values from -0.1875 to 0.1875
- tensor_mask: int32 [4, 8, 8], P('aux', 'ao'), may hold values 0 or 1
- green_mask: int32 [8, 8], P('aux', 'ao'), may hold values 0 or 1
Outputs:
- contracted: bfloat16 [64, 1024, 1024], P('aux', 'ao')
- polar: float32 [64, 16], P('aux')
All inputs are finite; a program needn't handle non-finite values. No bound on the sum of `tensor_mask` or of `green_mask` on one device may be relied on, other than what follows from the above.
Results may differ from a plain program's by a relative error of at most 0.001.
Values may be sent and summed in bfloat16 or wider, within the bound.
A program may use at most 128 MiB of HBM per device.

v0:
```python
import jax
import jax.numpy as jnp
from jax import lax
from jax.sharding import PartitionSpec as P

BLK = 128


def expand_blocks(mask, width):
    return jnp.repeat(jnp.repeat(mask, width, axis=0), width, axis=1)


def local(tensor, green, tensor_mask, green_mask):
    aux_count, row_count, orbitals = tensor.shape
    masked = tensor * expand_blocks(tensor_mask[0], BLK).astype(jnp.bfloat16)[None]
    green_local = green * expand_blocks(green_mask, BLK).astype(jnp.bfloat16)
    columns = lax.all_gather(green_local, "aux", axis=0, tiled=True)
    product = jnp.einsum(
        "pmn,nk->pmk",
        masked,
        lax.all_gather(columns, "ao", axis=1, tiled=True),
        preferred_element_type=jnp.float32,
    )
    flat_product = product.reshape(aux_count, row_count * orbitals)
    flat_masked = masked.reshape(aux_count, row_count * orbitals).astype(jnp.float32)
    partial_polar = jnp.dot(flat_product, flat_masked.T, precision=lax.Precision.HIGHEST)
    polar = lax.psum(partial_polar, "ao") / orbitals
    return (product.astype(jnp.bfloat16), polar)


def solution(mesh):
    return jax.shard_map(
        local,
        mesh=mesh,
        in_specs=(P("aux", "ao", None), P("aux", "ao"), P("aux", "ao", None), P("aux", "ao")),
        out_specs=(P("aux", "ao", None), P("aux", None)),
        check_vma=False,
    )
```

profile of v0, /device:TPU:0, one launch (start us, length us, event | category | flops | bytes accessed | tf_op | source)
XLA Modules:
  0.0 101.3 jit_solution(9471934883735907705)
XLA Ops:
  7.2 0.0 all-gather.2.cloned.1.call-start
  7.2 0.7 convert_bitcast_fusion
  7.9 0.1 broadcast_bitcast_fusion.1
  7.9 0.9 broadcast_multiply_fusion.1
  8.9 16.3 %all_gather.6 = bf16[1024,128]{1,0:T(8,128)(2,1)} all-gather(bf16[256,128]{1,0:T(8,128)(2,1)S(1)} %broadcast_multiply_fusion.1), channel_id=1, replica_groups=mesh['aux'=4,'ao'=8] {'aux'}, dimensions={0}, use_global_device_ids=true | all-gather | bytes 327680 | tf_op jit(solution)/shard_map/all_gather | solution.py:17
  25.2 0.0 all-gather.2.cloned.1.call-update
  25.2 0.7 convert_bitcast_fusion.1
  25.9 0.1 broadcast_bitcast_fusion
  26.0 4.4 %broadcast_multiply_fusion = bf16[16,128,1024]{2,1,0:T(8,128)(2,1)} fusion(bf16[16,128,1024]{2,1,0:T(8,128)(2,1)} %param.4, bf16[1024]{0:T(1024)(128)(2,1)S(1)} %broadcast_bitcast_fusion), kind=kLoop, calls=%fused_computation.5 | loop fusion | flops 2097152 | bytes 8390656 | tf_op jit(solution)/shard_map/mul | solution.py:15
  30.4 24.8 %all-gather.2.cloned.1.call-done = bf16[1024,1024]{1,0:T(8,128)(2,1)} async-done(((bf16[1024,128]{1,0:T(8,128)(2,1)}), bf16[1024,1024]{1,0:T(8,128)(2,1)}) %all-gather.2.cloned.1.call-update) | async-done | bytes 2097168 | tf_op jit(solution)/shard_map/all_gather | solution.py:21
  55.1 0.0 copy-start
  55.2 9.5 %fusion.10 = (bf16[16,128,1024]{2,1,0:T(8,128)(2,1)}, f32[16,128,1024]{2,1,0:T(8,128)S(1)}) fusion(bf16[16,128,1024]{2,1,0:T(8,128)(2,1)} %broadcast_multiply_fusion, bf16[1024,1024]{1,0:T(8,128)(2,1)} %all-gather.2.cloned.1.call-done), kind=kOutput, calls=%fused_computation.13 | convolution fusion | flops 4297064448 | bytes 18874368 | tf_op jit(solution)/shard_map/pmn,nk->pmk/dot_general | solution.py:18
  64.7 0.0 copy-done
  64.7 15.8 %fusion.5 = f32[16,16]{1,0:T(8,128)S(1)} fusion(bf16[16,128,1024]{2,1,0:T(8,128)(2,1)S(1)} %copy-done, f32[16,128,1024]{2,1,0:T(8,128)S(1)} %get-tuple-element.3), kind=kOutput, calls=%fused_computation.6 | convolution fusion | flops 402653184 | bytes 12583936 | tf_op jit(solution)/shard_map/dot_general | solution.py:26
  80.5 13.4 %psum.7 = f32[16,16]{1,0:T(8,128)S(1)} all-reduce(f32[16,16]{1,0:T(8,128)S(1)} %fusion.5), channel_id=1, replica_groups=mesh['aux'=4,'ao'=8] {'ao'}, use_global_device_ids=true, to_apply=%region_0.0 | all-reduce | flops 256 | bytes 2048 | tf_op jit(solution)/shard_map/psum | solution.py:27
  93.9 0.6 broadcast_multiply_fusion.2
Async XLA Ops:
  7.2 48.0 %all-gather.2.cloned.1.call-start = ((), (), s32[]{:S(2)}) async-start(), calls=%async_computation | async-start | bytes 2359296 | tf_op jit(solution)/shard_map/all_gather | solution.py:21
  55.1 9.5 %copy-start = (bf16[16,128,1024]{2,1,0:T(8,128)(2,1)S(1)}, bf16[16,128,1024]{2,1,0:T(8,128)(2,1)}, u32[]{:S(2)}) copy-start(bf16[16,128,1024]{2,1,0:T(8,128)(2,1)} %broadcast_multiply_fusion) | copy-start | bytes 12582916
Sparse Core Ops, SparseCore 0:
  25.3 29.7 all-gather.1
where the time goes:
time: 102 us; the launch traced here: 101 us
  blocking collectives  29.7 us (29%)
  matrix products  25.3 us (25%)
  waiting for transfers between devices  24.8 us (24%)
  between operations  14 us (14%)
  other arithmetic  7.25 us (7%)
    all_gather x1, waiting for transfers between devices, local(): lax.all_gather(columns, 'ao', axis=1, tiled=True)  24.8 us
    all_gather x1, blocking collectives, local(): columns = lax.all_gather(green_local, 'aux', axis=0, tiled=True)  16.3 us
    dot_general x1, matrix products, local(): jnp.dot(flat_product, flat_masked.T, precision=lax.Precision.HIGHEST)  15.8 us
    psum x1, blocking collectives, local(): polar = lax.psum(partial_polar, 'ao') / orbitals  13.4 us
    dot_general x1, matrix products, local(): jnp.einsum('pmn,nk->pmk', masked, lax.all_gather(columns, 'ao', axis=1, t...  9.54 us
    mul x1, other arithmetic, local(): tensor * expand_blocks(tensor_mask[0], BLK).astype(jnp.bfloat16)[None]  4.39 us
  transfers between devices with their start and end apart: 1, of which 1 were waited for; matrix products, arithmetic and copies ran while one was open for 5% of the time, Pallas kernels for 0%

commit v1 on v0

--- a/solution.py
+++ b/solution.py
@@ -4,6 +4,19 @@
 from jax.sharding import PartitionSpec as P
 
 BLK = 128
+
+
+def ring_gather(array, axis, dim):
+    size, here, extent = (lax.axis_size(axis), lax.axis_index(axis), array.shape[dim])
+    upward = [(i, (i + 1) % size) for i in range(size)]
+    out = jnp.zeros((*array.shape[:dim], size * extent, *array.shape[dim + 1 :]), array.dtype)
+    current = array
+    for step in range(size):
+        owner = (here - step) % size
+        out = lax.dynamic_update_slice_in_dim(out, current, owner * extent, axis=dim)
+        if step < size - 1:
+            current = lax.ppermute(current, axis, upward)
+    return out
 
 
 def expand_blocks(mask, width):
@@ -16,10 +29,7 @@
     green_local = green * expand_blocks(green_mask, BLK).astype(jnp.bfloat16)
     columns = lax.all_gather(green_local, "aux", axis=0, tiled=True)
     product = jnp.einsum(
-        "pmn,nk->pmk",
-        masked,
-        lax.all_gather(columns, "ao", axis=1, tiled=True),
-        preferred_element_type=jnp.float32,
+        "pmn,nk->pmk", masked, ring_gather(columns, "ao", 1), preferred_element_type=jnp.float32
     )
     flat_product = product.reshape(aux_count, row_count * orbitals)
     flat_masked = masked.reshape(aux_count, row_count * orbitals).astype(jnp.float32)

time: 102 us -> 99.8 us (0.978)
  waiting for transfers between devices: 24.8 us -> 40.7 us
  between operations: 14 us -> 0.74 us
  matrix products: 25.3 us -> 21.9 us
  blocking collectives: 29.7 us -> 27.7 us
    ppermute x0 -> x7, waiting for transfers between devices: none -> 40.7 us  [ring_gather(): current = lax.ppermute(current, axis, upward)]
    all_gather x1 -> x0, waiting for transfers between devices: 24.8 us -> none  [local(): lax.all_gather(columns, 'ao', axis=1, tiled=True)]
    dot_general x1, matrix products: 9.54 us -> 6.09 us  [local(): jnp.einsum('pmn,nk->pmk', masked, ring_gather(columns, 'ao', 1), preferre...]
    psum x1, blocking collectives: 13.4 us -> 12.1 us  [local(): polar = lax.psum(partial_polar, 'ao') / orbitals]
  transfers between devices with their start and end apart: 1 -> 7, of which waited for: 1 -> 7; matrix products, arithmetic and copies ran while one was open for 5% -> 6% of each run, Pallas kernels for 0% -> 0%
where the time goes in v1:
time: 99.8 us; the launch traced here: 99.5 us
  waiting for transfers between devices  40.7 us (41%)
  blocking collectives  27.7 us (28%)
  matrix products  21.9 us (22%)
  other arithmetic  7.33 us (7%)
  local copies, waits for them, and re-layouts  1.1 us (1%)
    ppermute x7, waiting for transfers between devices, ring_gather(): current = lax.ppermute(current, axis, upward)  40.7 us
    dot_general x1, matrix products, local(): jnp.dot(flat_product, flat_masked.T, precision=lax.Precision.HIGHEST)  15.8 us
    all_gather x1, blocking collectives, local(): columns = lax.all_gather(green_local, 'aux', axis=0, tiled=True)  15.6 us
    psum x1, blocking collectives, local(): polar = lax.psum(partial_polar, 'ao') / orbitals  12.1 us
    dot_general x1, matrix products, local(): jnp.einsum('pmn,nk->pmk', masked, ring_gather(columns, 'ao', 1), preferre...  6.09 us
    mul x1, other arithmetic, local(): tensor * expand_blocks(tensor_mask[0], BLK).astype(jnp.bfloat16)[None]  4.47 us
  transfers between devices with their start and end apart: 7, of which 7 were waited for; matrix products, arithmetic and copies ran while one was open for 6% of the time, Pallas kernels for 0%

profile of v1, /device:TPU:0, one launch (start us, length us, event | category | flops | bytes accessed | tf_op | source)
XLA Modules:
  0.0 99.5 jit_solution(9172508954560843679)
XLA Ops:
  0.6 0.7 convert_bitcast_fusion
  1.3 0.1 broadcast_bitcast_fusion.1
  1.4 0.9 broadcast_multiply_fusion.1
  2.3 15.6 %all_gather.3 = bf16[1024,128]{1,0:T(8,128)(2,1)S(1)} all-gather(bf16[256,128]{1,0:T(8,128)(2,1)S(1)} %broadcast_multiply_fusion.1), channel_id=1, replica_groups=mesh['aux'=4,'ao'=8] {'aux'}, dimensions={0}, use_global_device_ids=true | all-gather | bytes 327680 | tf_op jit(solution)/shard_map/all_gather | solution.py:30
  17.9 0.0 collective-permute-start
  17.9 6.7 %collective-permute-done = bf16[1024,128]{1,0:T(8,128)(2,1)S(1)} collective-permute-done((bf16[1024,128]{1,0:T(8,128)(2,1)S(1)}, bf16[1024,128]{1,0:T(8,128)(2,1)S(1)}, u32[]{:S(2)}, u32[]{:S(2)}) %collective-permute-start) | collective-permute-done | bytes 262176 | tf_op jit(solution)/shard_map/ppermute | solution.py:18
  24.6 0.0 collective-permute-start.1
  24.6 6.7 %collective-permute-done.1 = bf16[1024,128]{1,0:T(8,128)(2,1)S(1)} collective-permute-done((bf16[1024,128]{1,0:T(8,128)(2,1)S(1)}, bf16[1024,128]{1,0:T(8,128)(2,1)S(1)}, u32[]{:S(2)}, u32[]{:S(2)}) %collective-permute-start.1) | collective-permute-done | bytes 262176 | tf_op jit(solution)/shard_map/ppermute | solution.py:18
  31.3 0.0 collective-permute-start.2
  31.3 6.7 %collective-permute-done.2 = bf16[1024,128]{1,0:T(8,128)(2,1)S(1)} collective-permute-done((bf16[1024,128]{1,0:T(8,128)(2,1)S(1)}, bf16[1024,128]{1,0:T(8,128)(2,1)S(1)}, u32[]{:S(2)}, u32[]{:S(2)}) %collective-permute-start.2) | collective-permute-done | bytes 262176 | tf_op jit(solution)/shard_map/ppermute | solution.py:18
  38.0 0.0 collective-permute-start.3
  38.0 0.7 convert_bitcast_fusion.1
  38.7 0.1 broadcast_bitcast_fusion
  38.8 6.0 %collective-permute-done.3 = bf16[1024,128]{1,0:T(8,128)(2,1)S(1)} collective-permute-done((bf16[1024,128]{1,0:T(8,128)(2,1)S(1)}, bf16[1024,128]{1,0:T(8,128)(2,1)S(1)}, u32[]{:S(2)}, u32[]{:S(2)}) %collective-permute-start.3) | collective-permute-done | bytes 262176 | tf_op jit(solution)/shard_map/ppermute | solution.py:18
  44.7 0.0 collective-permute-start.4
  44.7 4.5 %broadcast_multiply_fusion = bf16[16,128,1024]{2,1,0:T(8,128)(2,1)} fusion(bf16[16,128,1024]{2,1,0:T(8,128)(2,1)} %param.4, bf16[1024]{0:T(1024)(128)(2,1)S(1)} %broadcast_bitcast_fusion), kind=kLoop, calls=%fused_computation.5 | loop fusion | flops 2097152 | bytes 8390656 | tf_op jit(solution)/shard_map/mul | solution.py:28
  49.2 0.3 broadcast_in_dim.13
  49.5 0.0 copy-start
  49.5 0.1 constant_dynamic-update-slice_fusion.7
  49.6 1.9 %collective-permute-done.4 = bf16[1024,128]{1,0:T(8,128)(2,1)S(1)} collective-permute-done((bf16[1024,128]{1,0:T(8,128)(2,1)S(1)}, bf16[1024,128]{1,0:T(8,128)(2,1)S(1)}, u32[]{:S(2)}, u32[]{:S(2)}) %collective-permute-start.4) | collective-permute-done | bytes 262176 | tf_op jit(solution)/shard_map/ppermute | solution.py:18
  51.4 0.0 collective-permute-start.5
  51.4 0.1 constant_dynamic-update-slice_fusion.6
  51.5 0.1 constant_dynamic-update-slice_fusion.5
  51.6 0.1 constant_dynamic-update-slice_fusion.4
  51.7 6.4 %collective-permute-done.5 = bf16[1024,128]{1,0:T(8,128)(2,1)S(1)} collective-permute-done((bf16[1024,128]{1,0:T(8,128)(2,1)S(1)}, bf16[1024,128]{1,0:T(8,128)(2,1)S(1)}, u32[]{:S(2)}, u32[]{:S(2)}) %collective-permute-start.5) | collective-permute-done | bytes 262176 | tf_op jit(solution)/shard_map/ppermute | solution.py:18
  58.1 0.0 collective-permute-start.6
  58.1 0.1 constant_dynamic-update-slice_fusion.3
  58.2 0.1 constant_dynamic-update-slice_fusion.2
  58.3 0.1 constant_dynamic-update-slice_fusion.1
  58.4 6.4 %collective-permute-done.6 = bf16[1024,128]{1,0:T(8,128)(2,1)S(1)} collective-permute-done((bf16[1024,128]{1,0:T(8,128)(2,1)S(1)}, bf16[1024,128]{1,0:T(8,128)(2,1)S(1)}, u32[]{:S(2)}, u32[]{:S(2)}) %collective-permute-start.6) | collective-permute-done | bytes 262176 | tf_op jit(solution)/shard_map/ppermute | solution.py:18
  64.8 0.1 constant_dynamic-update-slice_fusion
  64.9 0.0 copy-done
  64.9 6.1 %fusion.10 = (bf16[16,128,1024]{2,1,0:T(8,128)(2,1)}, f32[16,128,1024]{2,1,0:T(8,128)S(1)}) fusion(bf16[16,128,1024]{2,1,0:T(8,128)(2,1)S(1)} %copy-done, bf16[1024,1024]{1,0:T(8,128)(2,1)S(1)} %constant_dynamic-update-slice_fusion), kind=kOutput, calls=%fused_computation.21 | convolution fusion | flops 4297064448 | bytes 18874368 | tf_op jit(solution)/shard_map/pmn,nk->pmk/dot_general | solution.py:31
  71.0 15.8 %fusion.5 = f32[16,16]{1,0:T(8,128)S(1)} fusion(bf16[16,128,1024]{2,1,0:T(8,128)(2,1)S(1)} %copy-done, f32[16,128,1024]{2,1,0:T(8,128)S(1)} %get-tuple-element.3), kind=kOutput, calls=%fused_computation.6 | convolution fusion | flops 402653184 | bytes 12583936 | tf_op jit(solution)/shard_map/dot_general | solution.py:36
  86.8 12.1 %psum.7 = f32[16,16]{1,0:T(8,128)S(1)} all-reduce(f32[16,16]{1,0:T(8,128)S(1)} %fusion.5), channel_id=1, replica_groups=mesh['aux'=4,'ao'=8] {'ao'}, use_global_device_ids=true, to_apply=%region_0.1 | all-reduce | flops 256 | bytes 2048 | tf_op jit(solution)/shard_map/psum | solution.py:37
  98.9 0.6 broadcast_multiply_fusion.2
Async XLA Ops:
  17.9 6.7 %collective-permute-start = (bf16[1024,128]{1,0:T(8,128)(2,1)S(1)}, bf16[1024,128]{1,0:T(8,128)(2,1)S(1)}, u32[]{:S(2)}, u32[]{:S(2)}) collective-permute-start(bf16[1024,128]{1,0:T(8,128)(2,1)S(1)} %all_gather.3), channel_id=1, source_target_pairs={{0,1},{1,2},{2,3},{3,4},{4,5},{5,6},{6,7},{7,0},{8,9},{9,10},{10,1... | collective-permute-start | bytes 786440 | tf_op jit(solution)/shard_map/ppermute | solution.py:18
  24.6 6.7 %collective-permute-start.1 = (bf16[1024,128]{1,0:T(8,128)(2,1)S(1)}, bf16[1024,128]{1,0:T(8,128)(2,1)S(1)}, u32[]{:S(2)}, u32[]{:S(2)}) collective-permute-start(bf16[1024,128]{1,0:T(8,128)(2,1)S(1)} %collective-permute-done), channel_id=1, source_target_pairs={{0,1},{1,2},{2,3},{3,4},{4,5},{5,6},{6,7},{7,0},{8,9},{9,10},{10,1... | collective-permute-start | bytes 786440 | tf_op jit(solution)/shard_map/ppermute | solution.py:18
  31.3 6.7 %collective-permute-start.2 = (bf16[1024,128]{1,0:T(8,128)(2,1)S(1)}, bf16[1024,128]{1,0:T(8,128)(2,1)S(1)}, u32[]{:S(2)}, u32[]{:S(2)}) collective-permute-start(bf16[1024,128]{1,0:T(8,128)(2,1)S(1)} %collective-permute-done.1), channel_id=1, source_target_pairs={{0,1},{1,2},{2,3},{3,4},{4,5},{5,6},{6,7},{7,0},{8,9},{9,10},{10,1... | collective-permute-start | bytes 786440 | tf_op jit(solution)/shard_map/ppermute | solution.py:18
  38.0 6.7 %collective-permute-start.3 = (bf16[1024,128]{1,0:T(8,128)(2,1)S(1)}, bf16[1024,128]{1,0:T(8,128)(2,1)S(1)}, u32[]{:S(2)}, u32[]{:S(2)}) collective-permute-start(bf16[1024,128]{1,0:T(8,128)(2,1)S(1)} %collective-permute-done.2), channel_id=1, source_target_pairs={{0,1},{1,2},{2,3},{3,4},{4,5},{5,6},{6,7},{7,0},{8,9},{9,10},{10,1... | collective-permute-start | bytes 786440 | tf_op jit(solution)/shard_map/ppermute | solution.py:18
  44.7 6.7 %collective-permute-start.4 = (bf16[1024,128]{1,0:T(8,128)(2,1)S(1)}, bf16[1024,128]{1,0:T(8,128)(2,1)S(1)}, u32[]{:S(2)}, u32[]{:S(2)}) collective-permute-start(bf16[1024,128]{1,0:T(8,128)(2,1)S(1)} %collective-permute-done.3), channel_id=1, source_target_pairs={{0,1},{1,2},{2,3},{3,4},{4,5},{5,6},{6,7},{7,0},{8,9},{9,10},{10,1... | collective-permute-start | bytes 786440 | tf_op jit(solution)/shard_map/ppermute | solution.py:18
  49.5 15.4 %copy-start = (bf16[16,128,1024]{2,1,0:T(8,128)(2,1)S(1)}, bf16[16,128,1024]{2,1,0:T(8,128)(2,1)}, u32[]{:S(2)}) copy-start(bf16[16,128,1024]{2,1,0:T(8,128)(2,1)} %broadcast_multiply_fusion) | copy-start | bytes 12582916
  51.4 6.7 %collective-permute-start.5 = (bf16[1024,128]{1,0:T(8,128)(2,1)S(1)}, bf16[1024,128]{1,0:T(8,128)(2,1)S(1)}, u32[]{:S(2)}, u32[]{:S(2)}) collective-permute-start(bf16[1024,128]{1,0:T(8,128)(2,1)S(1)} %collective-permute-done.4), channel_id=1, source_target_pairs={{0,1},{1,2},{2,3},{3,4},{4,5},{5,6},{6,7},{7,0},{8,9},{9,10},{10,1... | collective-permute-start | bytes 786440 | tf_op jit(solution)/shard_map/ppermute | solution.py:18
  58.1 6.7 %collective-permute-start.6 = (bf16[1024,128]{1,0:T(8,128)(2,1)S(1)}, bf16[1024,128]{1,0:T(8,128)(2,1)S(1)}, u32[]{:S(2)}, u32[]{:S(2)}) collective-permute-start(bf16[1024,128]{1,0:T(8,128)(2,1)S(1)} %collective-permute-done.5), channel_id=1, source_target_pairs={{0,1},{1,2},{2,3},{3,4},{4,5},{5,6},{6,7},{7,0},{8,9},{9,10},{10,1... | collective-permute-start | bytes 786440 | tf_op jit(solution)/shard_map/ppermute | solution.py:18

commit v2 on v0

--- a/solution.py
+++ b/solution.py
@@ -24,7 +24,7 @@
     flat_product = product.reshape(aux_count, row_count * orbitals)
     flat_masked = masked.reshape(aux_count, row_count * orbitals).astype(jnp.float32)
     partial_polar = jnp.dot(flat_product, flat_masked.T, precision=lax.Precision.HIGHEST)
-    polar = lax.psum(partial_polar, "ao") / orbitals
+    polar = jnp.sum(lax.all_gather(partial_polar, "ao"), axis=0) / orbitals
     return (product.astype(jnp.bfloat16), polar)
 
 

time: 102 us -> 97.4 us (0.955)
  blocking collectives: 29.7 us -> 25.5 us
    psum x1 -> x0, blocking collectives: 13.4 us -> none  [local(): polar = lax.psum(partial_polar, 'ao') / orbitals]
    all_gather x0 -> x1, blocking collectives: none -> 9.21 us  [local(): polar = jnp.sum(lax.all_gather(partial_polar, 'ao'), axis=0) / orbitals]
where the time goes in v2:
time: 97.4 us; the launch traced here: 97.2 us
  blocking collectives  25.5 us (26%)
  matrix products  25.3 us (26%)
  waiting for transfers between devices  24.8 us (25%)
  between operations  14 us (14%)
  other arithmetic  7.26 us (7%)
    all_gather x1, waiting for transfers between devices, local(): lax.all_gather(columns, 'ao', axis=1, tiled=True)  24.8 us
    all_gather x1, blocking collectives, local(): columns = lax.all_gather(green_local, 'aux', axis=0, tiled=True)  16.3 us
    dot_general x1, matrix products, local(): jnp.dot(flat_product, flat_masked.T, precision=lax.Precision.HIGHEST)  15.8 us
    dot_general x1, matrix products, local(): jnp.einsum('pmn,nk->pmk', masked, lax.all_gather(columns, 'ao', axis=1, t...  9.54 us
    all_gather x1, blocking collectives, local(): polar = jnp.sum(lax.all_gather(partial_polar, 'ao'), axis=0) / orbitals  9.21 us
    mul x1, other arithmetic, local(): tensor * expand_blocks(tensor_mask[0], BLK).astype(jnp.bfloat16)[None]  4.39 us
  transfers between devices with their start and end apart: 1, of which 1 were waited for; matrix products, arithmetic and copies ran while one was open for 5% of the time, Pallas kernels for 0%

profile of v2, /device:TPU:0, one launch (start us, length us, event | category | flops | bytes accessed | tf_op | source)
XLA Modules:
  0.0 97.2 jit_solution(3464120384544892419)
XLA Ops:
  7.2 0.0 all-gather.3.cloned.1.call-start
  7.2 0.7 convert_bitcast_fusion
  7.9 0.1 broadcast_bitcast_fusion.1
  7.9 0.9 broadcast_multiply_fusion.1
  8.9 16.3 %all_gather.12 = bf16[1024,128]{1,0:T(8,128)(2,1)} all-gather(bf16[256,128]{1,0:T(8,128)(2,1)S(1)} %broadcast_multiply_fusion.1), channel_id=1, replica_groups=mesh['aux'=4,'ao'=8] {'aux'}, dimensions={0}, use_global_device_ids=true | all-gather | bytes 327680 | tf_op jit(solution)/shard_map/all_gather | solution.py:17
  25.2 0.0 all-gather.3.cloned.1.call-update
  25.2 0.7 convert_bitcast_fusion.1
  25.9 0.1 broadcast_bitcast_fusion
  26.0 4.4 %broadcast_multiply_fusion = bf16[16,128,1024]{2,1,0:T(8,128)(2,1)} fusion(bf16[16,128,1024]{2,1,0:T(8,128)(2,1)} %param.4, bf16[1024]{0:T(1024)(128)(2,1)S(1)} %broadcast_bitcast_fusion), kind=kLoop, calls=%fused_computation.5 | loop fusion | flops 2097152 | bytes 8390656 | tf_op jit(solution)/shard_map/mul | solution.py:15
  30.4 24.8 %all-gather.3.cloned.1.call-done = bf16[1024,1024]{1,0:T(8,128)(2,1)} async-done(((bf16[1024,128]{1,0:T(8,128)(2,1)}), bf16[1024,1024]{1,0:T(8,128)(2,1)}) %all-gather.3.cloned.1.call-update) | async-done | bytes 2097168 | tf_op jit(solution)/shard_map/all_gather | solution.py:21
  55.1 0.0 copy-start
  55.2 9.5 %fusion.10 = (bf16[16,128,1024]{2,1,0:T(8,128)(2,1)}, f32[16,128,1024]{2,1,0:T(8,128)S(1)}) fusion(bf16[16,128,1024]{2,1,0:T(8,128)(2,1)} %broadcast_multiply_fusion, bf16[1024,1024]{1,0:T(8,128)(2,1)} %all-gather.3.cloned.1.call-done), kind=kOutput, calls=%fused_computation.13 | convolution fusion | flops 4297064448 | bytes 18874368 | tf_op jit(solution)/shard_map/pmn,nk->pmk/dot_general | solution.py:18
  64.7 0.0 copy-done
  64.7 15.8 %fusion.5 = f32[16,16]{1,0:T(8,128)S(1)} fusion(bf16[16,128,1024]{2,1,0:T(8,128)(2,1)S(1)} %copy-done, f32[16,128,1024]{2,1,0:T(8,128)S(1)} %get-tuple-element.3), kind=kOutput, calls=%fused_computation.6 | convolution fusion | flops 402653184 | bytes 12583936 | tf_op jit(solution)/shard_map/dot_general | solution.py:26
  80.5 9.2 %all-gather = f32[128,16]{1,0:T(8,128)S(1)} all-gather(f32[16,16]{1,0:T(8,128)S(1)} %fusion.5), channel_id=2, replica_groups=mesh['aux'=4,'ao'=8] {'ao'}, dimensions={0}, use_global_device_ids=true | all-gather | bytes 9216 | tf_op jit(solution)/shard_map/all_gather | solution.py:27
  89.7 0.6 broadcast_multiply_fusion.2
  (1 shorter events, 0.0 us)
Async XLA Ops:
  7.2 48.0 %all-gather.3.cloned.1.call-start = ((), (), s32[]{:S(2)}) async-start(), calls=%async_computation | async-start | bytes 2359296 | tf_op jit(solution)/shard_map/all_gather | solution.py:21
  55.1 9.5 %copy-start = (bf16[16,128,1024]{2,1,0:T(8,128)(2,1)S(1)}, bf16[16,128,1024]{2,1,0:T(8,128)(2,1)}, u32[]{:S(2)}) copy-start(bf16[16,128,1024]{2,1,0:T(8,128)(2,1)} %broadcast_multiply_fusion) | copy-start | bytes 12582916
Sparse Core Ops, SparseCore 0:
  25.3 29.7 all-gather.2
